TPU v7x, 32 devices: a whole 2x2x4 slice. The times are simulated.
32 devices in a mesh: dom: 8 (over z, x), feat: 4 (over y, core).
Axes of the slice: x: 2, y: 2, z: 4, core: 2. Of those that a mesh axis runs over, the one named last changes fastest.
Arguments:
- features: bfloat16 [768, 16384], P('feat', 'dom'), may hold values from -6 to 6
- neighbors: int32 [16, 16384], P(None, 'dom'), may hold values from 0 to 3071
- degree: int32 [16384], P('dom'), may hold values from 1 to 16
- send_rows: int32 [8, 8, 128], P('dom'), may hold values from 0 to 2047
- labels: int32 [16384], P('dom'), may hold values from 0 to 1
- w_self: bfloat16 [768, 512], replicated, may hold values from -0.21875 to 0.21875
- w_neigh: bfloat16 [768, 512], replicated, may hold values from -0.21875 to 0.21875
- bias: float32 [512], replicated, may hold values from -3 to 3
- a_self: float32 [512], replicated, may hold values from -0.5 to 0.5
- a_neigh: float32 [512], replicated, may hold values from -0.5 to 0.5
Outputs:
- logits: float32 [16384], P('dom')
- grad_self: float32 [768, 512], P('feat')
- grad_neigh: float32 [768, 512], P('feat')
Inputs may be any that keep to these rules, and one draw needn't show every extreme that they name: `neighbors`: slots under 2048 are the partition's own nodes, the others nodes sent by other partitions.
All inputs are finite; a program needn't handle non-finite values.
Results may differ from a plain program's by a relative error of at most 0.012.
The roundings to bfloat16 on the way count: a program that leaves them out, or rounds other values in their place, can miss the bound.
Values may be sent and summed in bfloat16 or wider, within the bound.
A program may use at most 128 MiB of HBM per device.

v0:
```python
import jax
import jax.numpy as jnp
from jax import lax
from jax.sharding import PartitionSpec as P


def body(features, neighbors, degree, send_rows, labels, w_self, w_neigh, bias, a_self, a_neigh):
    partitions = lax.axis_size("dom")
    slices = lax.axis_size("feat")
    node_count = features.shape[1]
    block_rows = node_count // slices
    column_count = features.shape[0]
    fan_slots = neighbors.shape[0]
    send_local = send_rows[0].reshape(-1)
    neighbor_mask = jnp.arange(fan_slots)[:, None] < degree[None, :]
    inverse = 1.0 / degree.astype(jnp.float32)
    outgoing = features[:, send_local]
    incoming = lax.all_to_all(outgoing, "dom", split_axis=1, concat_axis=1, tiled=True)
    table = jnp.concatenate([features, incoming], axis=1)
    summed = jnp.zeros((column_count, node_count), jnp.float32)
    for neighbor_slot in range(fan_slots):
        taken = table[:, neighbors[neighbor_slot]].astype(jnp.float32)
        summed = summed + jnp.where(neighbor_mask[neighbor_slot][None, :], taken, 0.0)
    aggregated = (summed * inverse[None, :]).astype(jnp.bfloat16)
    feature_block, aggregate_block = (
        lax.all_to_all(features, "feat", split_axis=1, concat_axis=0, tiled=True),
        lax.all_to_all(aggregated, "feat", split_axis=1, concat_axis=0, tiled=True),
    )
    dims = (((0,), (0,)), ((), ()))
    preact = (
        lax.dot_general(feature_block, w_self, dims, preferred_element_type=jnp.float32)
        + lax.dot_general(aggregate_block, w_neigh, dims, preferred_element_type=jnp.float32)
        + bias
    )
    hidden = jnp.maximum(preact, 0.0)
    block_self = jnp.sum(hidden * a_self, axis=1)
    block_neigh = jnp.sum(hidden * a_neigh, axis=1)
    score_self, score_neigh = (
        lax.all_gather(block_self, "feat", axis=0, tiled=True),
        lax.all_gather(block_neigh, "feat", axis=0, tiled=True),
    )
    score_out = score_neigh[send_local]
    score_in = lax.all_to_all(score_out, "dom", split_axis=0, concat_axis=0, tiled=True)
    score_table = jnp.concatenate([score_neigh, score_in], axis=0)
    logits = (
        score_self
        + jnp.sum(jnp.where(neighbor_mask, score_table[neighbors], 0.0), axis=0) * inverse
    )
    loss_scale = float(node_count * partitions) ** (-0.5)
    dlogit = (jax.nn.sigmoid(logits) - labels.astype(jnp.float32)) * loss_scale
    weighted = jnp.where(neighbor_mask, (dlogit * inverse)[None, :], 0.0)
    slot_grads = jnp.zeros((score_table.shape[0],), jnp.float32).at[neighbors].add(weighted)
    boundary_out = slot_grads[node_count:]
    returned = lax.all_to_all(boundary_out, "dom", split_axis=0, concat_axis=0, tiled=True)
    dneigh = slot_grads[:node_count].at[send_local].add(returned)
    slice_index = lax.axis_index("feat")
    dlogit_block = lax.dynamic_slice_in_dim(dlogit, slice_index * block_rows, block_rows, 0)
    dneigh_block = lax.dynamic_slice_in_dim(dneigh, slice_index * block_rows, block_rows, 0)
    dpre = jnp.where(
        preact > 0, dlogit_block[:, None] * a_self + dneigh_block[:, None] * a_neigh, 0.0
    ).astype(jnp.bfloat16)
    piece = lax.all_gather(dpre, "feat", axis=0, tiled=True)
    local_self = jnp.dot(features, piece, preferred_element_type=jnp.float32)
    local_neigh = jnp.dot(aggregated, piece, preferred_element_type=jnp.float32)
    grad_self, grad_neigh = lax.psum((local_self, local_neigh), "dom")
    return (logits, grad_self, grad_neigh)


def solution(mesh):
    return jax.shard_map(
        body,
        mesh=mesh,
        in_specs=(
            P("feat", "dom"),
            P(None, "dom"),
            P("dom"),
            P("dom", None, None),
            P("dom"),
            P(),
            P(),
            P(),
            P(),
            P(),
        ),
        out_specs=(P("dom"), P("feat", None), P("feat", None)),
        check_vma=False,
    )
```

profile of v0, /device:TPU:0, one launch (start us, length us, event | category | flops | bytes accessed | tf_op | source)
XLA Modules:
  0.0 808.3 jit_solution(845162668443788434)
XLA Ops:
  9.4 3.9 gather_fusion
  14.3 7.3 all-to-all-start.1
  43.1 4.4 all-to-all-start
  49.8 8.5 %gather_fusion.1 = bf16[2048,192]{1,0:T(8,128)(2,1)S(1)} fusion(bf16[192,3072]{0,1:T(8,128)(2,1)S(1)} %pad_maximum_fusion, s32[2048]{0:T(1024)} %broadcast_clamp_fusion.16), kind=kCustom, calls=%fused_computation.1 | custom fusion | bytes 1581056 | tf_op jit(solution)/shard_map/gather | solution.py:22
  58.3 1.7 convert_element_type.228
  60.0 2.8 copy.57
  62.8 8.5 %gather_fusion.2 = bf16[2048,192]{1,0:T(8,128)(2,1)S(1)} fusion(bf16[192,3072]{0,1:T(8,128)(2,1)S(1)} %pad_maximum_fusion, s32[2048]{0:T(1024)} %broadcast_clamp_fusion.15), kind=kCustom, calls=%fused_computation.2 | custom fusion | bytes 1581056 | tf_op jit(solution)/shard_map/gather | solution.py:22
  71.3 1.7 convert_element_type.229
  73.0 2.8 copy.58
  75.7 8.5 %gather_fusion.3 = bf16[2048,192]{1,0:T(8,128)(2,1)S(1)} fusion(bf16[192,3072]{0,1:T(8,128)(2,1)S(1)} %pad_maximum_fusion, s32[2048]{0:T(1024)} %broadcast_clamp_fusion.14), kind=kCustom, calls=%fused_computation.3 | custom fusion | bytes 1581056 | tf_op jit(solution)/shard_map/gather | solution.py:22
  85.9 2.8 copy.59
  88.7 8.5 %gather_fusion.4 = bf16[2048,192]{1,0:T(8,128)(2,1)S(1)} fusion(bf16[192,3072]{0,1:T(8,128)(2,1)S(1)} %pad_maximum_fusion, s32[2048]{0:T(1024)} %broadcast_clamp_fusion.13), kind=kCustom, calls=%fused_computation.4 | custom fusion | bytes 1581056 | tf_op jit(solution)/shard_map/gather | solution.py:22
  97.2 1.7 convert_element_type.231
  98.9 2.8 copy.60
  101.7 8.5 %gather_fusion.5 = bf16[2048,192]{1,0:T(8,128)(2,1)S(1)} fusion(bf16[192,3072]{0,1:T(8,128)(2,1)S(1)} %pad_maximum_fusion, s32[2048]{0:T(1024)} %broadcast_clamp_fusion.12), kind=kCustom, calls=%fused_computation.5 | custom fusion | bytes 1581056 | tf_op jit(solution)/shard_map/gather | solution.py:22
  110.2 1.7 convert_element_type.232
  111.9 2.7 copy.61
  114.6 8.5 %gather_fusion.6 = bf16[2048,192]{1,0:T(8,128)(2,1)S(1)} fusion(bf16[192,3072]{0,1:T(8,128)(2,1)S(1)} %pad_maximum_fusion, s32[2048]{0:T(1024)} %broadcast_clamp_fusion.11), kind=kCustom, calls=%fused_computation.6 | custom fusion | bytes 1581056 | tf_op jit(solution)/shard_map/gather | solution.py:22
  123.1 1.7 convert_element_type.233
  124.8 2.7 copy.62
  127.5 8.5 %gather_fusion.7 = bf16[2048,192]{1,0:T(8,128)(2,1)S(1)} fusion(bf16[192,3072]{0,1:T(8,128)(2,1)S(1)} %pad_maximum_fusion, s32[2048]{0:T(1024)} %broadcast_clamp_fusion.10), kind=kCustom, calls=%fused_computation.7 | custom fusion | bytes 1581056 | tf_op jit(solution)/shard_map/gather | solution.py:22
  137.7 2.8 copy.63
  140.5 8.5 %gather_fusion.8 = bf16[2048,192]{1,0:T(8,128)(2,1)S(1)} fusion(bf16[192,3072]{0,1:T(8,128)(2,1)S(1)} %pad_maximum_fusion, s32[2048]{0:T(1024)} %broadcast_clamp_fusion.9), kind=kCustom, calls=%fused_computation.8 | custom fusion | bytes 1581056 | tf_op jit(solution)/shard_map/gather | solution.py:22
  150.7 2.8 copy.64
  153.5 8.5 %gather_fusion.9 = bf16[2048,192]{1,0:T(8,128)(2,1)S(1)} fusion(bf16[192,3072]{0,1:T(8,128)(2,1)S(1)} %pad_maximum_fusion, s32[2048]{0:T(1024)} %broadcast_clamp_fusion.8), kind=kCustom, calls=%fused_computation.9 | custom fusion | bytes 1581056 | tf_op jit(solution)/shard_map/gather | solution.py:22
  162.0 1.7 convert_element_type.236
  163.7 2.8 copy.65
  166.4 8.5 %gather_fusion.10 = bf16[2048,192]{1,0:T(8,128)(2,1)S(1)} fusion(bf16[192,3072]{0,1:T(8,128)(2,1)S(1)} %pad_maximum_fusion, s32[2048]{0:T(1024)} %broadcast_clamp_fusion.7), kind=kCustom, calls=%fused_computation.10 | custom fusion | bytes 1581056 | tf_op jit(solution)/shard_map/gather | solution.py:22
  174.9 1.7 convert_element_type.237
  176.6 2.8 copy.66
  179.4 8.5 %gather_fusion.11 = bf16[2048,192]{1,0:T(8,128)(2,1)S(1)} fusion(bf16[192,3072]{0,1:T(8,128)(2,1)S(1)} %pad_maximum_fusion, s32[2048]{0:T(1024)} %broadcast_clamp_fusion.6), kind=kCustom, calls=%fused_computation.11 | custom fusion | bytes 1581056 | tf_op jit(solution)/shard_map/gather | solution.py:22
  187.9 1.7 convert_element_type.238
  189.6 2.8 copy.67
  192.3 8.5 %gather_fusion.12 = bf16[2048,192]{1,0:T(8,128)(2,1)S(1)} fusion(bf16[192,3072]{0,1:T(8,128)(2,1)S(1)} %pad_maximum_fusion, s32[2048]{0:T(1024)} %broadcast_clamp_fusion.5), kind=kCustom, calls=%fused_computation.12 | custom fusion | bytes 1581056 | tf_op jit(solution)/shard_map/gather | solution.py:22
  202.5 2.8 copy.68
  205.3 8.5 %gather_fusion.13 = bf16[2048,192]{1,0:T(8,128)(2,1)S(1)} fusion(bf16[192,3072]{0,1:T(8,128)(2,1)S(1)} %pad_maximum_fusion, s32[2048]{0:T(1024)} %broadcast_clamp_fusion.4), kind=kCustom, calls=%fused_computation.13 | custom fusion | bytes 1581056 | tf_op jit(solution)/shard_map/gather | solution.py:22
  215.5 2.7 copy.69
  218.3 8.5 %gather_fusion.14 = bf16[2048,192]{1,0:T(8,128)(2,1)S(1)} fusion(bf16[192,3072]{0,1:T(8,128)(2,1)S(1)} %pad_maximum_fusion, s32[2048]{0:T(1024)} %broadcast_clamp_fusion.3), kind=kCustom, calls=%fused_computation.14 | custom fusion | bytes 1581056 | tf_op jit(solution)/shard_map/gather | solution.py:22
  228.5 2.8 copy.70
  231.2 8.7 %gather_fusion.15 = bf16[2048,192]{1,0:T(8,128)(2,1)S(1)} fusion(bf16[192,3072]{0,1:T(8,128)(2,1)S(1)} %pad_maximum_fusion, s32[2048]{0:T(1024)} %broadcast_clamp_fusion.2), kind=kCustom, calls=%fused_computation.15 | custom fusion | bytes 1581056 | tf_op jit(solution)/shard_map/gather | solution.py:22
  241.6 2.8 copy.71
  244.4 9.0 %gather_fusion.16 = bf16[2048,192]{1,0:T(8,128)(2,1)} fusion(bf16[192,3072]{0,1:T(8,128)(2,1)S(1)} %pad_maximum_fusion, s32[2048]{0:T(1024)S(1)} %copy-done.26), kind=kCustom, calls=%fused_computation.16 | custom fusion | bytes 1581056 | tf_op jit(solution)/shard_map/gather | solution.py:22
  255.0 1.7 copy.72
  256.8 12.7 %multiply_convert_fusion = bf16[192,4,512]{2,0,1:T(8,128)(2,1)} fusion(f32[192,4,512]{2,0,1:T(8,128)} %copy.72, f32[192,4,512]{2,0,1:T(8,128)} %copy.71, f32[192,4,512]{2,0,1:T(8,128)} %copy.70, f32[192,4,512]{2,0,1:T(8,128)} %copy.69, f32[192,4,512]{2,0,1:T(8,128)} %copy.68, f32[192,4,512]{2,0,1:T(8,128)} %copy.67, f32[192,4,512]{2,0,1:T(8,128)} %copy.66, ...), kind=kLoop, calls=%fused_computation.55 | loop fusion | flops 12976128 | bytes 25993216 | tf_op jit(solution)/shard_map/convert_element_type | solution.py:24
  269.5 3.6 all-to-all-start.2
  273.2 1.7 fusion.41
  275.0 9.8 %all-to-all-done.2 = bf16[192,4,512]{2,0,1:T(8,128)(2,1)S(1)} async-done(((bf16[192,4,512]{2,0,1:T(8,128)(2,1)}), bf16[192,4,512]{2,0,1:T(8,128)(2,1)S(1)}, u32[]{:S(2)}, u32[]{:S(2)}) %all-to-all-start.2) | async-done | bytes 786464 | tf_op jit(solution)/shard_map/all_to_all | solution.py:27
  284.8 2.5 multiply_reduce_fusion
  287.2 5.1 all-gather.1
  292.4 10.5 %gather_fusion.17 = f32[1024]{0:T(1024)} fusion(f32[2048]{0:T(1024)S(1)} %bitcast.235, s32[1024]{0:T(1024)S(1)} %broadcast_clamp_fusion.17), kind=kCustom, calls=%fused_computation.17 | custom fusion | bytes 12288 | tf_op jit(solution)/shard_map/gather | solution.py:42
  302.9 6.0 all-to-all-start.3
  308.9 5.2 all-gather
  315.3 180.5 %gather_fusion.18 = f32[32768]{0:T(1024)S(1)} fusion(f32[3072]{0:T(1024)S(1)} %pad_maximum_fusion.1, s32[32768]{0:T(1024)S(1)} %broadcast_clamp_fusion), kind=kCustom, calls=%fused_computation.18 | custom fusion | bytes 393216 | tf_op jit(solution)/shard_map/gather | solution.py:47
  496.6 171.0 %scatter_custom_fusion = f32[3072]{0:T(1024)S(1)} fusion(s32[32768]{0:T(1024)S(1)} %bitcast.258, f32[32768]{0:T(1024)S(1)} %bitcast.259, f32[]{:T(128)} %constant.11.clone.1), kind=kCustom, calls=%fused_computation.123 | custom fusion | flops 32768 | bytes 12292 | tf_op jit(solution)/shard_map/scatter-add | solution.py:52
  668.2 4.8 all-to-all-start.4
  673.2 6.2 all-to-all-done.4
  679.5 6.1 scatter_fusion
  685.8 2.4 select_convert_fusion
  688.3 19.1 %all-gather.4.cloned.1.call-done = bf16[2048,512]{0,1:T(8,128)(2,1)} async-done(((bf16[512,512]{0,1:T(8,128)(2,1)}), bf16[2048,512]{0,1:T(8,128)(2,1)}) %all-gather.4.cloned.1.call-update) | async-done | bytes 2097168 | tf_op jit(solution)/shard_map/all_gather | solution.py:62
  707.5 12.5 %fusion.18 = f32[192,512]{1,0:T(8,128)} fusion(bf16[2048,512]{0,1:T(8,128)(2,1)} %all-gather.4.cloned.1.call-done, f32[2048]{0:T(1024)S(1)} %copy-done.25, pred[2048]{0:T(1024)(128)(4,1)S(1)} %copy-done.30, pred[2048]{0:T(1024)(128)(4,1)S(1)} %copy-done.32, pred[2048]{0:T(1024)(128)(4,1)S(1)} %copy-done.34, pred[2048]{0:T(1024)(128)(4,1)S(1)} %copy-done.36, ...), kind=kOutput, calls=%fused_computation.62 | convolution fusion | flops 421920768 | bytes 15114240 | tf_op jit(solution)/shard_map/dot_general | solution.py:64
  720.0 2.8 convolution_bitcast_fusion
  722.9 75.0 %all-reduce.3.cloned.1.call-done = (f32[192,512]{1,0:T(8,128)}, f32[192,512]{1,0:T(8,128)}) async-done(((f32[192,512]{1,0:T(8,128)}, f32[192,512]{1,0:T(8,128)}), (f32[192,512]{1,0:T(8,128)}, f32[192,512]{1,0:T(8,128)})) %all-reduce.3.cloned.1.call-update) | async-done | bytes 786448 | tf_op jit(solution)/shard_map/psum | solution.py:65
  797.9 1.8 copy.83
  799.7 1.8 copy.84
  (230 shorter events, 43.2 us)
Async XLA Ops:
  7.2 277.6 %copy-start = (bf16[768,512]{1,0:T(8,128)(2,1)S(1)}, bf16[768,512]{1,0:T(8,128)(2,1)}, u32[]{:S(2)}) copy-start(bf16[768,512]{1,0:T(8,128)(2,1)} %param.16) | copy-start | bytes 2359300
  13.3 8.2 %copy-start.22 = (s32[2048]{0:T(1024)S(1)}, s32[2048]{0:T(1024)}, u32[]{:S(2)}) copy-start(s32[2048]{0:T(1024)} %param.12) | copy-start | bytes 24580
  13.4 8.3 %copy-start.21 = (s32[16,2048]{1,0:T(8,128)S(1)}, s32[16,2048]{1,0:T(8,128)}, u32[]{:S(2)}) copy-start(s32[16,2048]{1,0:T(8,128)} %param.11) | copy-start | bytes 393220
  13.4 26.7 %copy-start.19 = (bf16[192,2048]{1,0:T(8,128)(2,1)S(1)}, bf16[192,2048]{1,0:T(8,128)(2,1)}, u32[]{:S(2)}) copy-start(bf16[192,2048]{1,0:T(8,128)(2,1)} %param.10) | copy-start | bytes 2359300
  14.3 28.6 %all-to-all-start.1 = ((bf16[192,8,128]{2,0,1:T(8,128)(2,1)}), bf16[192,8,128]{2,0,1:T(8,128)(2,1)S(1)}, u32[]{:S(2)}, u32[]{:S(2)}) async-start(bf16[192,8,128]{2,0,1:T(8,128)(2,1)} %copy.54), calls=%async_computation.1 | async-start | bytes 786432 | tf_op jit(solution)/shard_map/all_to_all | solution.py:18
  21.6 21.3 %copy-start.24 = (f32[2048]{0:T(1024)}, f32[2048]{0:T(1024)S(1)}, u32[]{:S(2)}) copy-start(f32[2048]{0:T(1024)S(1)} %convert_divide_fusion) | copy-start | bytes 24580
  30.0 13.0 %copy-start.27 = (pred[2048]{0:T(1024)(128)(4,1)}, pred[2048]{0:T(1024)(128)(4,1)S(1)}, u32[]{:S(2)}) copy-start(pred[2048]{0:T(1024)(128)(4,1)S(1)} %get-tuple-element.5) | copy-start | bytes 6148
  30.0 12.9 %copy-start.29 = (pred[2048]{0:T(1024)(128)(4,1)}, pred[2048]{0:T(1024)(128)(4,1)S(1)}, u32[]{:S(2)}) copy-start(pred[2048]{0:T(1024)(128)(4,1)S(1)} %get-tuple-element.6) | copy-start | bytes 6148
  30.0 12.9 %copy-start.31 = (pred[2048]{0:T(1024)(128)(4,1)}, pred[2048]{0:T(1024)(128)(4,1)S(1)}, u32[]{:S(2)}) copy-start(pred[2048]{0:T(1024)(128)(4,1)S(1)} %get-tuple-element.7) | copy-start | bytes 6148
  30.0 12.9 %copy-start.33 = (pred[2048]{0:T(1024)(128)(4,1)}, pred[2048]{0:T(1024)(128)(4,1)S(1)}, u32[]{:S(2)}) copy-start(pred[2048]{0:T(1024)(128)(4,1)S(1)} %get-tuple-element.8) | copy-start | bytes 6148
  30.0 12.9 %copy-start.35 = (pred[2048]{0:T(1024)(128)(4,1)}, pred[2048]{0:T(1024)(128)(4,1)S(1)}, u32[]{:S(2)}) copy-start(pred[2048]{0:T(1024)(128)(4,1)S(1)} %get-tuple-element.9) | copy-start | bytes 6148
  30.0 12.9 %copy-start.37 = (pred[2048]{0:T(1024)(128)(4,1)}, pred[2048]{0:T(1024)(128)(4,1)S(1)}, u32[]{:S(2)}) copy-start(pred[2048]{0:T(1024)(128)(4,1)S(1)} %get-tuple-element.10) | copy-start | bytes 6148
  30.0 12.9 %copy-start.39 = (pred[2048]{0:T(1024)(128)(4,1)}, pred[2048]{0:T(1024)(128)(4,1)S(1)}, u32[]{:S(2)}) copy-start(pred[2048]{0:T(1024)(128)(4,1)S(1)} %get-tuple-element.11) | copy-start | bytes 6148
  30.0 12.9 %copy-start.41 = (pred[2048]{0:T(1024)(128)(4,1)}, pred[2048]{0:T(1024)(128)(4,1)S(1)}, u32[]{:S(2)}) copy-start(pred[2048]{0:T(1024)(128)(4,1)S(1)} %get-tuple-element.12) | copy-start | bytes 6148
  30.0 12.9 %copy-start.43 = (pred[2048]{0:T(1024)(128)(4,1)}, pred[2048]{0:T(1024)(128)(4,1)S(1)}, u32[]{:S(2)}) copy-start(pred[2048]{0:T(1024)(128)(4,1)S(1)} %get-tuple-element.13) | copy-start | bytes 6148
  30.0 12.9 %copy-start.45 = (pred[2048]{0:T(1024)(128)(4,1)}, pred[2048]{0:T(1024)(128)(4,1)S(1)}, u32[]{:S(2)}) copy-start(pred[2048]{0:T(1024)(128)(4,1)S(1)} %get-tuple-element.14) | copy-start | bytes 6148
  30.1 12.9 %copy-start.47 = (pred[2048]{0:T(1024)(128)(4,1)}, pred[2048]{0:T(1024)(128)(4,1)S(1)}, u32[]{:S(2)}) copy-start(pred[2048]{0:T(1024)(128)(4,1)S(1)} %get-tuple-element.15) | copy-start | bytes 6148
  30.1 12.9 %copy-start.49 = (pred[2048]{0:T(1024)(128)(4,1)}, pred[2048]{0:T(1024)(128)(4,1)S(1)}, u32[]{:S(2)}) copy-start(pred[2048]{0:T(1024)(128)(4,1)S(1)} %get-tuple-element.16) | copy-start | bytes 6148
  30.1 12.9 %copy-start.51 = (pred[2048]{0:T(1024)(128)(4,1)}, pred[2048]{0:T(1024)(128)(4,1)S(1)}, u32[]{:S(2)}) copy-start(pred[2048]{0:T(1024)(128)(4,1)S(1)} %get-tuple-element.17) | copy-start | bytes 6148
  30.1 12.9 %copy-start.53 = (pred[2048]{0:T(1024)(128)(4,1)}, pred[2048]{0:T(1024)(128)(4,1)S(1)}, u32[]{:S(2)}) copy-start(pred[2048]{0:T(1024)(128)(4,1)S(1)} %get-tuple-element.18) | copy-start | bytes 6148
  30.1 12.9 %copy-start.55 = (pred[2048]{0:T(1024)(128)(4,1)}, pred[2048]{0:T(1024)(128)(4,1)S(1)}, u32[]{:S(2)}) copy-start(pred[2048]{0:T(1024)(128)(4,1)S(1)} %get-tuple-element.19) | copy-start | bytes 6148
  30.1 12.9 %copy-start.57 = (pred[2048]{0:T(1024)(128)(4,1)}, pred[2048]{0:T(1024)(128)(4,1)S(1)}, u32[]{:S(2)}) copy-start(pred[2048]{0:T(1024)(128)(4,1)S(1)} %get-tuple-element.20) | copy-start | bytes 6148
  43.1 226.4 %all-to-all-start = ((bf16[192,4,512]{2,0,1:T(8,128)(2,1)}), bf16[192,4,512]{2,0,1:T(8,128)(2,1)}, u32[]{:S(2)}, u32[]{:S(2)}) async-start(bf16[192,4,512]{2,0,1:T(8,128)(2,1)} %bitcast.234), calls=%async_computation | async-start | bytes 1572864 | tf_op jit(solution)/shard_map/all_to_all | solution.py:26
  241.6 2.8 copy-start.26
  254.8 1.9 copy-start.23
  254.8 1.9 copy-start.59
  254.8 1.8 copy-start.60
  254.8 1.8 copy-start.61
  254.8 1.8 copy-start.62
  254.9 1.8 copy-start.63
  254.9 1.8 copy-start.64
  254.9 1.8 copy-start.65
  254.9 1.8 copy-start.66
  254.9 1.8 copy-start.67
  269.5 3.7 copy-start.20
  269.5 15.3 %all-to-all-start.2 = ((bf16[192,4,512]{2,0,1:T(8,128)(2,1)}), bf16[192,4,512]{2,0,1:T(8,128)(2,1)S(1)}, u32[]{:S(2)}, u32[]{:S(2)}) async-start(bf16[192,4,512]{2,0,1:T(8,128)(2,1)} %multiply_convert_fusion), calls=%async_computation.2 | async-start | bytes 1572864 | tf_op jit(solution)/shard_map/all_to_all | solution.py:27
  302.9 12.4 %all-to-all-start.3 = ((f32[8,128,1]{1,2,0:T(1,128)}), f32[8,128,1]{1,2,0:T(1,128)S(1)}, u32[]{:S(2)}, u32[]{:S(2)}) async-start(f32[8,128,1]{1,2,0:T(1,128)} %bitcast.78), calls=%async_computation.3 | async-start | bytes 8192 | tf_op jit(solution)/shard_map/all_to_all | solution.py:43
  315.3 180.6 %copy-start.75 = (s32[2048]{0:T(1024)S(1)}, s32[2048]{0:T(1024)}, u32[]{:S(2)}) copy-start(s32[2048]{0:T(1024)} %param.14) | copy-start | bytes 24580
  668.2 11.2 %all-to-all-start.4 = ((f32[8,128,1]{1,2,0:T(1,128)}), f32[8,128,1]{1,2,0:T(1,128)S(1)}, u32[]{:S(2)}, u32[]{:S(2)}) async-start(f32[8,128,1]{1,2,0:T(1,128)} %bitcast.81), calls=%async_computation.4 | async-start | bytes 8192 | tf_op jit(solution)/shard_map/all_to_all | solution.py:54
  673.1 34.3 %all-gather.4.cloned.1.call-start = ((), (), s32[]{:S(2)}) async-start(), calls=%async_computation.5 | async-start | bytes 2621440 | tf_op jit(solution)/shard_map/all_gather | solution.py:62
  679.4 6.4 copy-start.76
  679.4 6.4 copy-start.77
  679.5 27.9 %copy-start.38 = (pred[2048]{0:T(1024)(128)(4,1)S(1)}, pred[2048]{0:T(1024)(128)(4,1)}, u32[]{:S(2)}) copy-start(pred[2048]{0:T(1024)(128)(4,1)} %copy-done.37) | copy-start | bytes 6148
  679.5 27.9 %copy-start.40 = (pred[2048]{0:T(1024)(128)(4,1)S(1)}, pred[2048]{0:T(1024)(128)(4,1)}, u32[]{:S(2)}) copy-start(pred[2048]{0:T(1024)(128)(4,1)} %copy-done.39) | copy-start | bytes 6148
  679.5 27.9 %copy-start.42 = (pred[2048]{0:T(1024)(128)(4,1)S(1)}, pred[2048]{0:T(1024)(128)(4,1)}, u32[]{:S(2)}) copy-start(pred[2048]{0:T(1024)(128)(4,1)} %copy-done.41) | copy-start | bytes 6148
  679.5 27.9 %copy-start.44 = (pred[2048]{0:T(1024)(128)(4,1)S(1)}, pred[2048]{0:T(1024)(128)(4,1)}, u32[]{:S(2)}) copy-start(pred[2048]{0:T(1024)(128)(4,1)} %copy-done.43) | copy-start | bytes 6148
  679.5 27.9 %copy-start.46 = (pred[2048]{0:T(1024)(128)(4,1)S(1)}, pred[2048]{0:T(1024)(128)(4,1)}, u32[]{:S(2)}) copy-start(pred[2048]{0:T(1024)(128)(4,1)} %copy-done.45) | copy-start | bytes 6148
  679.5 27.9 %copy-start.48 = (pred[2048]{0:T(1024)(128)(4,1)S(1)}, pred[2048]{0:T(1024)(128)(4,1)}, u32[]{:S(2)}) copy-start(pred[2048]{0:T(1024)(128)(4,1)} %copy-done.47) | copy-start | bytes 6148
  679.5 27.9 %copy-start.50 = (pred[2048]{0:T(1024)(128)(4,1)S(1)}, pred[2048]{0:T(1024)(128)(4,1)}, u32[]{:S(2)}) copy-start(pred[2048]{0:T(1024)(128)(4,1)} %copy-done.49) | copy-start | bytes 6148
  679.5 27.9 %copy-start.52 = (pred[2048]{0:T(1024)(128)(4,1)S(1)}, pred[2048]{0:T(1024)(128)(4,1)}, u32[]{:S(2)}) copy-start(pred[2048]{0:T(1024)(128)(4,1)} %copy-done.51) | copy-start | bytes 6148
  679.5 27.9 %copy-start.54 = (pred[2048]{0:T(1024)(128)(4,1)S(1)}, pred[2048]{0:T(1024)(128)(4,1)}, u32[]{:S(2)}) copy-start(pred[2048]{0:T(1024)(128)(4,1)} %copy-done.53) | copy-start | bytes 6148
  679.5 27.9 %copy-start.56 = (pred[2048]{0:T(1024)(128)(4,1)S(1)}, pred[2048]{0:T(1024)(128)(4,1)}, u32[]{:S(2)}) copy-start(pred[2048]{0:T(1024)(128)(4,1)} %copy-done.55) | copy-start | bytes 6148
  679.5 27.9 %copy-start.58 = (pred[2048]{0:T(1024)(128)(4,1)S(1)}, pred[2048]{0:T(1024)(128)(4,1)}, u32[]{:S(2)}) copy-start(pred[2048]{0:T(1024)(128)(4,1)} %copy-done.57) | copy-start | bytes 6148
  685.6 21.8 %copy-start.3 = (bf16[2048,192]{1,0:T(8,128)(2,1)S(1)}, bf16[2048,192]{1,0:T(8,128)(2,1)}, u32[]{:S(2)}) copy-start(bf16[2048,192]{1,0:T(8,128)(2,1)} %copy-done.2) | copy-start | bytes 2359300
  685.7 21.8 %copy-start.5 = (bf16[2048,192]{1,0:T(8,128)(2,1)S(1)}, bf16[2048,192]{1,0:T(8,128)(2,1)}, u32[]{:S(2)}) copy-start(bf16[2048,192]{1,0:T(8,128)(2,1)} %copy-done.4) | copy-start | bytes 2359300
  685.7 21.8 %copy-start.25 = (f32[2048]{0:T(1024)S(1)}, f32[2048]{0:T(1024)}, u32[]{:S(2)}) copy-start(f32[2048]{0:T(1024)} %copy-done.24) | copy-start | bytes 24580
  685.7 21.8 %copy-start.28 = (pred[2048]{0:T(1024)(128)(4,1)S(1)}, pred[2048]{0:T(1024)(128)(4,1)}, u32[]{:S(2)}) copy-start(pred[2048]{0:T(1024)(128)(4,1)} %copy-done.27) | copy-start | bytes 6148
  685.7 21.8 %copy-start.30 = (pred[2048]{0:T(1024)(128)(4,1)S(1)}, pred[2048]{0:T(1024)(128)(4,1)}, u32[]{:S(2)}) copy-start(pred[2048]{0:T(1024)(128)(4,1)} %copy-done.29) | copy-start | bytes 6148
  685.7 21.8 %copy-start.32 = (pred[2048]{0:T(1024)(128)(4,1)S(1)}, pred[2048]{0:T(1024)(128)(4,1)}, u32[]{:S(2)}) copy-start(pred[2048]{0:T(1024)(128)(4,1)} %copy-done.31) | copy-start | bytes 6148
  685.7 21.8 %copy-start.34 = (pred[2048]{0:T(1024)(128)(4,1)S(1)}, pred[2048]{0:T(1024)(128)(4,1)}, u32[]{:S(2)}) copy-start(pred[2048]{0:T(1024)(128)(4,1)} %copy-done.33) | copy-start | bytes 6148
  685.7 21.8 %copy-start.36 = (pred[2048]{0:T(1024)(128)(4,1)S(1)}, pred[2048]{0:T(1024)(128)(4,1)}, u32[]{:S(2)}) copy-start(pred[2048]{0:T(1024)(128)(4,1)} %copy-done.35) | copy-start | bytes 6148
  688.2 109.7 %all-reduce.3.cloned.1.call-start = ((), (), s32[]{:S(2)}) async-start(), calls=%async_computation.6 | async-start | bytes 1572864 | tf_op jit(solution)/shard_map/psum | solution.py:65
  707.5 12.5 %copy-start.78 = (bf16[2048,512]{0,1:T(8,128)(2,1)S(1)}, bf16[2048,512]{0,1:T(8,128)(2,1)}, u32[]{:S(2)}) copy-start(bf16[2048,512]{0,1:T(8,128)(2,1)} %all-gather.4.cloned.1.call-done) | copy-start | bytes 6291460
  720.0 81.4 %copy-start.1 = (bf16[768,512]{1,0:T(8,128)(2,1)S(1)}, bf16[768,512]{1,0:T(8,128)(2,1)}, u32[]{:S(2)}) copy-start(bf16[768,512]{1,0:T(8,128)(2,1)} %param.16) | copy-start | bytes 2359300
  (22 other events, 38.6 us)
Sparse Core Ops, SparseCore 0:
  688.4 18.9 all-gather.3
  723.0 74.8 all-reduce.2
where the time goes:
time: 811 us; the launch traced here: 808 us
  local copies, waits for them, and re-layouts  394 us (49%)
  other arithmetic  231 us (28%)
  waiting for transfers between devices  111 us (14%)
  starting transfers between devices  26.2 us (3%)
  matrix products  19.5 us (2%)
  between operations  15.3 us (2%)
  blocking collectives  10.3 us (1%)
    gather x2, local copies, waits for them, and re-layouts, body(): score_table[neighbors]  181 us
    scatter-add x1, other arithmetic, body(): jnp.zeros((score_table.shape[0],), jnp.float32).at[neighbors].add(weighted)  171 us
    gather x16, local copies, waits for them, and re-layouts, body(): taken = table[:, neighbors[neighbor_slot]].astype(jnp.float32)  136 us
    psum x1, waiting for transfers between devices, body(): grad_self, grad_neigh = lax.psum((local_self, local_neigh), 'dom')  75 us
    convert_element_type x16, local copies, waits for them, and re-layouts, body(): taken = table[:, neighbors[neighbor_slot]].astype(jnp.float32)  43.2 us
    convert_element_type x16, other arithmetic, body(): taken = table[:, neighbors[neighbor_slot]].astype(jnp.float32)  26.5 us
    all_gather x1, waiting for transfers between devices, body(): piece = lax.all_gather(dpre, 'feat', axis=0, tiled=True)  19.1 us
  transfers between devices with their start and end apart: 7, of which 5 were waited for; matrix products, arithmetic and copies ran while one was open for 30% of the time, Pallas kernels for 0%

commit v1 on v0

v1 whole, which is shorter than its diff:
```python
import functools

import jax
import jax.numpy as jnp
from jax import lax
from jax.experimental import pallas as pl
from jax.experimental.pallas import tpu as pltpu
from jax.sharding import PartitionSpec as P

MESH = pl.DeviceIdType.MESH
BF = jnp.bfloat16
F32 = jnp.float32
NN = (((1,), (0,)), ((), ()))
NT = (((1,), (1,)), ((), ()))
TN = (((0,), (0,)), ((), ()))
GROUPS = 6
BITS = 5


def dot(a, b, dims):
    return lax.dot_general(a, b, dims, preferred_element_type=F32)


def split(row):
    wide = jnp.broadcast_to(row, (16, row.shape[1]))
    sub = lax.broadcasted_iota(jnp.int32, wide.shape, 0)
    first = wide.astype(BF).astype(F32)
    rest = wide - first
    second = rest.astype(BF).astype(F32)
    third = rest - second
    out = jnp.where(sub == 0, first, jnp.where(sub == 1, second, jnp.where(sub == 2, third, 0.0)))
    return out.astype(BF)


def total(rows):
    return jnp.sum(rows, axis=0, keepdims=True)


def kernel(
    parts, slices, reduce_here, scale,
    feat_ref, neigh_ref, degree_ref, send_ref, label_ref, ws_ref, wn_ref, bias_ref, as_ref, an_ref,
    logit_ref, gself_ref, gneigh_ref,
    hi_ref, val_ref, count_ref, pick_ref, fblk_ref, ablk_ref, agg_ref, out_ref, inc_ref, inctab_ref,
    col_ref, pre_ref, mask_ref, score_ref, srow_ref, sout_ref, sin_ref, stab_ref, wsplit_ref, slot_ref,
    gout_ref, gin_ref, back_ref, dn_ref, dl_ref, acc_ref, dpre_ref, rs_out, rs_in, ag_ref,
    feat_send, feat_recv, dom_send, dom_recv,
):
    d = lax.axis_index("dom")
    f = lax.axis_index("feat")
    cols, nodes = feat_ref.shape
    fan = neigh_ref.shape[0]
    remote = send_ref.shape[1]
    table = nodes + remote
    each = remote // parts
    block = nodes // slices
    hid = ws_ref.shape[1]
    rows = table // GROUPS
    shift = rows.bit_length() - 1

    barrier = pltpu.get_barrier_semaphore()
    for j in range(1, parts):
        pl.semaphore_signal(barrier, inc=1, device_id={"dom": lax.rem(d + j, parts)}, device_id_type=MESH)
    for j in range(1, slices):
        pl.semaphore_signal(barrier, inc=1, device_id={"feat": lax.rem(f + j, slices)}, device_id_type=MESH)
    pl.semaphore_wait(barrier, parts + slices - 2)

    sent = []

    def feat_copy(phase, j, src, dst):
        copy = pltpu.make_async_remote_copy(
            src_ref=src, dst_ref=dst, send_sem=feat_send.at[phase, j], recv_sem=feat_recv.at[phase, j],
            device_id={"feat": lax.rem(f + j, slices)}, device_id_type=MESH)
        copy.start()
        sent.append(copy)

    def dom_copy(phase, j, src, dst):
        copy = pltpu.make_async_remote_copy(
            src_ref=src, dst_ref=dst, send_sem=dom_send.at[phase, j], recv_sem=dom_recv.at[phase, j],
            device_id={"dom": lax.rem(d + j, parts)}, device_id_type=MESH)
        copy.start()
        sent.append(copy)

    def feat_wait(phase, j, dst):
        pltpu.make_async_remote_copy(
            src_ref=dst, dst_ref=dst, send_sem=feat_send.at[phase, j], recv_sem=feat_recv.at[phase, j],
            device_id={"feat": lax.rem(f + j, slices)}, device_id_type=MESH).wait_recv()

    def dom_wait(phase, j, dst):
        pltpu.make_async_remote_copy(
            src_ref=dst, dst_ref=dst, send_sem=dom_send.at[phase, j], recv_sem=dom_recv.at[phase, j],
            device_id={"dom": lax.rem(d + j, parts)}, device_id_type=MESH).wait_recv()

    def feat_peer(j):
        return lax.rem(f + j, slices)

    def feat_from(j):
        return lax.rem(f + slices - j, slices)

    def dom_peer(j):
        return lax.rem(d + j, parts)

    def dom_from(j):
        return lax.rem(d + parts - j, parts)

    def span(index):
        return pl.ds(pl.multiple_of(index * block, block), block)

    step = min(256, remote)

    def pick(i, _):
        r = pl.multiple_of(i * 256, 256)
        here = lax.broadcasted_iota(jnp.int32, (256, remote), 0) + r
        pick_ref[pl.ds(r, 256), :] = jnp.where(here == send_ref[...], 1.0, 0.0).astype(BF)
        return 0

    lax.fori_loop(0, nodes // 256, pick, 0)
    for c in range(remote // step):
        got = dot(feat_ref[...], pick_ref[:, c * step:(c + 1) * step], NN).astype(BF)
        for p in range(step // each):
            out_ref[c * (step // each) + p] = got[:, p * each:(p + 1) * each]
    for j in range(1, parts):
        dom_copy(0, j, out_ref.at[dom_peer(j)], inc_ref.at[d])
    inc_ref[d] = out_ref[d]

    for j in range(1, slices):
        feat_copy(0, j, feat_ref.at[:, span(feat_peer(j))], fblk_ref.at[f])
    fblk_ref[f] = feat_ref[:, span(f)]

    slot = lax.broadcasted_iota(jnp.int32, (fan, nodes), 0)
    used = slot < degree_ref[...]
    hi_ref[...] = neigh_ref[...] & (rows - 1)
    val_ref[...] = jnp.where(used, jnp.left_shift(jnp.int32(1), (neigh_ref[...] >> shift) * BITS), 0)

    def count_lanes(c, _):
        lanes = pl.ds(pl.multiple_of(c * 128, 128), 128)
        his = [jnp.broadcast_to(hi_ref[k:k + 1, lanes], (16, 128)) for k in range(fan)]
        vals = [jnp.broadcast_to(val_ref[k:k + 1, lanes], (16, 128)) for k in range(fan)]
        base = lax.broadcasted_iota(jnp.int32, (16, 128), 0)

        def count_rows(i, _):
            r = pl.multiple_of(i * 16, 16)
            here = base + r
            terms = [jnp.where(h == here, v, 0) for h, v in zip(his, vals)]
            while len(terms) > 1:
                terms = [a + b for a, b in zip(terms[::2], terms[1::2])] + terms[len(terms) & ~1:]
            word = terms[0]
            for g in range(GROUPS):
                part = (word >> (BITS * g)) & ((1 << BITS) - 1)
                count_ref[pl.ds(pl.multiple_of(g * rows + r, 16), 16), lanes] = part.astype(F32).astype(BF)
            return 0

        lax.fori_loop(0, rows // 16, count_rows, 0)
        return 0

    lax.fori_loop(0, nodes // 128, count_lanes, 0)
    inverse = 1.0 / degree_ref[...].astype(F32)

    for k, ref in enumerate((bias_ref, as_ref, an_ref)):
        col_ref[k] = jnp.broadcast_to(ref[...], (128, hid)).T

    for j in range(1, parts):
        dom_wait(0, j, inc_ref.at[dom_from(j)])
    for p in range(parts):
        inctab_ref[:, p * each:(p + 1) * each] = inc_ref[p]

    tile = min(256, block)

    def aggregate(index):
        for t in range(block // tile):
            lanes = pl.ds(pl.multiple_of(index * block + t * tile, tile), tile)
            sums = dot(feat_ref[...], count_ref[:nodes, lanes], NN)
            sums = sums + dot(inctab_ref[...], count_ref[nodes:, lanes], NN)
            agg_ref[:, lanes] = (sums * (1.0 / degree_ref[:, lanes].astype(F32))).astype(BF)

    def aggregate_for(j, _):
        aggregate(lax.rem(f + j, slices))
        return 0

    for j in range(1, slices):
        aggregate(feat_peer(j))
        feat_copy(1, j, agg_ref.at[:, span(feat_peer(j))], ablk_ref.at[f])
    aggregate(f)
    ablk_ref[f] = agg_ref[:, span(f)]

    for j in range(1, slices):
        feat_wait(0, j, fblk_ref.at[feat_from(j)])
    depth = slices * cols
    pre_ref[...] = dot(ws_ref[...], fblk_ref[...].reshape(depth, block), TN)
    for j in range(1, slices):
        feat_wait(1, j, ablk_ref.at[feat_from(j)])
    pre_ref[...] += dot(wn_ref[...], ablk_ref[...].reshape(depth, block), TN)
    for t in range(block // 128):
        pre = pre_ref[:, t * 128:(t + 1) * 128] + col_ref[0]
        hidden = jnp.maximum(pre, 0.0)
        mask_ref[f, :, t * 128:(t + 1) * 128] = jnp.where(pre > 0, 1.0, 0.0).astype(BF)
        own = jnp.broadcast_to(total(hidden * col_ref[1]), (8, 128))
        other = jnp.broadcast_to(total(hidden * col_ref[2]), (8, 128))
        sub = lax.broadcasted_iota(jnp.int32, (8, 128), 0)
        score_ref[f, :, t * 128:(t + 1) * 128] = jnp.where(sub == 0, own, other)
    for j in range(1, slices):
        feat_copy(2, j, score_ref.at[f], score_ref.at[f])
    for j in range(1, slices):
        feat_copy(3, j, mask_ref.at[f], mask_ref.at[f])

    for j in range(1, slices):
        feat_wait(2, j, score_ref.at[feat_from(j)])
    for s in range(slices):
        srow_ref[:, s * block:(s + 1) * block] = score_ref[s]
    boundary = total(dot(split(srow_ref[1:2, :]), pick_ref[...], NN))
    for p in range(parts):
        sout_ref[p] = jnp.broadcast_to(boundary[:, p * each:(p + 1) * each], (8, each))
    for j in range(1, parts):
        dom_copy(1, j, sout_ref.at[dom_peer(j)], sin_ref.at[d])
    sin_ref[d] = sout_ref[d]
    stab_ref[:, :nodes] = jnp.broadcast_to(srow_ref[1:2, :], (8, nodes))
    for j in range(1, parts):
        dom_wait(1, j, sin_ref.at[dom_from(j)])
    for p in range(parts):
        stab_ref[:, nodes + p * each:nodes + (p + 1) * each] = sin_ref[p]

    spread = split(stab_ref[0:1, :])

    def logit_tile(i, _):
        lanes = pl.ds(pl.multiple_of(i * 256, 256), 256)
        slot_ref[0:1, lanes] = total(dot(spread, count_ref[:, lanes], NN))
        return 0

    lax.fori_loop(0, nodes // 256, logit_tile, 0)
    logits = srow_ref[0:1, :] + slot_ref[0:1, :nodes] * inverse
    logit_ref[...] = logits
    dlogit = (1.0 / (1.0 + jnp.exp(-logits)) - label_ref[...].astype(F32)) * scale
    dl_ref[...] = dlogit
    wsplit_ref[...] = split(dlogit * inverse)

    def slot_tile(i, _):
        lanes = pl.ds(pl.multiple_of(i * 256, 256), 256)
        slot_ref[0:1, lanes] = total(dot(wsplit_ref[...], count_ref[lanes, :], NT))
        return 0

    lax.fori_loop(nodes // 256, table // 256, slot_tile, 0)
    for p in range(parts):
        gout_ref[p] = jnp.broadcast_to(slot_ref[0:1, nodes + p * each:nodes + (p + 1) * each], (8, each))
    for j in range(1, parts):
        dom_copy(2, j, gout_ref.at[dom_peer(j)], gin_ref.at[d])
    gin_ref[d] = gout_ref[d]
    lax.fori_loop(0, nodes // 256, slot_tile, 0)
    for j in range(1, parts):
        dom_wait(2, j, gin_ref.at[dom_from(j)])
    for p in range(parts):
        back_ref[:, p * each:(p + 1) * each] = gin_ref[p]
    returned = split(back_ref[0:1, :])

    def back_tile(i, _):
        lanes = pl.ds(pl.multiple_of(i * 256, 256), 256)
        dn_ref[0:1, lanes] = slot_ref[0:1, lanes] + total(dot(returned, pick_ref[lanes, :], NT))
        return 0

    lax.fori_loop(0, nodes // 256, back_tile, 0)

    for j in range(slices):
        index = feat_from(j)
        if j:
            feat_wait(3, j, mask_ref.at[index])
        for t in range(block // 128):
            lanes = pl.ds(pl.multiple_of(index * block + t * 128, 128), 128)
            grad = dl_ref[:, lanes] * col_ref[1] + dn_ref[0:1, lanes] * col_ref[2]
            keep = mask_ref[index, :, t * 128:(t + 1) * 128].astype(F32)
            dpre_ref[:, t * 128:(t + 1) * 128] = jnp.where(keep > 0, grad, 0.0).astype(BF)
        own = dot(feat_ref[:, span(index)], dpre_ref[...], NT)
        other = dot(agg_ref[:, span(index)], dpre_ref[...], NT)
        if j:
            acc_ref[:cols] += own
            acc_ref[cols:] += other
        else:
            acc_ref[:cols] = own
            acc_ref[cols:] = other

    if reduce_here:
        share = 2 * cols // parts
        for p in range(parts):
            rs_out[p] = acc_ref[p * share:(p + 1) * share].astype(BF)
        for j in range(1, parts):
            dom_copy(3, j, rs_out.at[dom_peer(j)], rs_in.at[d])
        rs_in[d] = rs_out[d]
        for j in range(1, parts):
            dom_wait(3, j, rs_in.at[dom_from(j)])
        whole = rs_in[0].astype(F32)
        for p in range(1, parts):
            whole = whole + rs_in[p].astype(F32)
        ag_ref[d] = whole.astype(BF)
        for j in range(1, parts):
            dom_copy(4, j, ag_ref.at[d], ag_ref.at[d])
        for j in range(1, parts):
            dom_wait(4, j, ag_ref.at[dom_from(j)])
        for p in range(parts):
            ref = gself_ref if p < parts // 2 else gneigh_ref
            at = (p % (parts // 2)) * share
            ref[at:at + share] = ag_ref[p].astype(F32)
    else:
        gself_ref[...] = acc_ref[:cols]
        gneigh_ref[...] = acc_ref[cols:]
    for copy in sent:
        copy.wait_send()


def body(features, neighbors, degree, send_rows, labels, w_self, w_neigh, bias, a_self, a_neigh):
    parts = lax.axis_size("dom")
    slices = lax.axis_size("feat")
    cols, nodes = features.shape
    fan = neighbors.shape[0]
    each = send_rows.shape[2]
    remote = parts * each
    table = nodes + remote
    block = nodes // slices
    hid = w_self.shape[1]
    share = 2 * cols // parts
    reduce_here = parts % 2 == 0 and share * parts == 2 * cols and share % 16 == 0
    scale = float(nodes * parts) ** (-0.5)
    spare = share if reduce_here else 16
    V = pltpu.VMEM
    scratch = [
        V((fan, nodes), jnp.int32), V((fan, nodes), jnp.int32),
        V((table, nodes), BF), V((nodes, remote), BF),
        V((slices, cols, block), BF), V((slices, cols, block), BF), V((cols, nodes), BF),
        V((parts, cols, each), BF), V((parts, cols, each), BF), V((cols, remote), BF),
        V((3, hid, 128), F32), V((hid, block), F32), V((slices, hid, block), BF),
        V((slices, 8, block), F32), V((8, nodes), F32),
        V((parts, 8, each), F32), V((parts, 8, each), F32), V((8, table), F32),
        V((16, nodes), BF), V((8, table), F32),
        V((parts, 8, each), F32), V((parts, 8, each), F32), V((8, remote), F32),
        V((8, nodes), F32), V((1, nodes), F32),
        V((2 * cols, hid), F32), V((hid, block), BF),
        V((parts, spare, hid), BF), V((parts, spare, hid), BF), V((parts, spare, hid), BF),
        pltpu.SemaphoreType.DMA((4, slices)), pltpu.SemaphoreType.DMA((4, slices)),
        pltpu.SemaphoreType.DMA((5, parts)), pltpu.SemaphoreType.DMA((5, parts)),
    ]
    vm = pl.BlockSpec(memory_space=pltpu.VMEM)
    logits, grad_self, grad_neigh = pl.pallas_call(
        functools.partial(kernel, parts, slices, reduce_here, scale),
        out_shape=(
            jax.ShapeDtypeStruct((1, nodes), F32),
            jax.ShapeDtypeStruct((cols, hid), F32),
            jax.ShapeDtypeStruct((cols, hid), F32),
        ),
        in_specs=[vm] * 10,
        out_specs=(vm, vm, vm),
        scratch_shapes=scratch,
        compiler_params=pltpu.CompilerParams(
            collective_id=0, has_side_effects=True, vmem_limit_bytes=52 * 1024 * 1024),
    )(
        features, neighbors, degree.reshape(1, nodes), send_rows.reshape(1, remote), labels.reshape(1, nodes),
        w_self, w_neigh, bias.reshape(1, hid), a_self.reshape(1, hid), a_neigh.reshape(1, hid),
    )
    if not reduce_here:
        grad_self, grad_neigh = lax.psum((grad_self, grad_neigh), "dom")
    return (logits.reshape(nodes), grad_self, grad_neigh)


def solution(mesh):
    return jax.shard_map(
        body,
        mesh=mesh,
        in_specs=(
            P("feat", "dom"), P(None, "dom"), P("dom"), P("dom", None, None), P("dom"),
            P(), P(), P(), P(), P(),
        ),
        out_specs=(P("dom"), P("feat", None), P("feat", None)),
        check_vma=False,
    )
```

time: 811 us -> 82 us (0.10)
  the two profiles are of different devices: /device:TPU:0 before, /device:TPU:25 now
where the time goes in v1:
time: 82 us; the launch traced here: 81.6 us
  Pallas kernels  73.4 us (90%)
  local copies, waits for them, and re-layouts  7.56 us (9%)
    pallas_call x1, Pallas kernels, body(): pl.pallas_call(functools.partial(kernel, parts, slices, reduce_here, scal...  73.4 us
    unnamed x19, local copies, waits for them, and re-layouts  7.56 us

profile of v1, /device:TPU:25, one launch (start us, length us, event | category | flops | bytes accessed | tf_op | source)
XLA Modules:
  0.0 81.6 jit_solution(7021671866624231836)
XLA Ops:
  0.6 0.0 copy-start.2
  0.6 0.0 copy-start.5
  0.7 0.7 copy-done.2
  1.3 0.0 copy-done.5
  1.3 0.0 copy-start
  1.3 1.1 %copy-done = bf16[192,2048]{1,0:T(8,128)(2,1)S(1)} copy-done((bf16[192,2048]{1,0:T(8,128)(2,1)S(1)}, bf16[192,2048]{1,0:T(8,128)(2,1)}, u32[]{:S(2)}) %copy-start) | copy-done | bytes 786456
  2.5 0.0 copy-start.1
  2.5 0.9 %copy-done.1 = s32[16,2048]{1,0:T(8,128)S(1)} copy-done((s32[16,2048]{1,0:T(8,128)S(1)}, s32[16,2048]{1,0:T(8,128)}, u32[]{:S(2)}) %copy-start.1) | copy-done | bytes 131096
  3.4 0.0 copy-start.3
  3.4 0.7 copy-done.3
  4.1 0.0 copy-start.4
  4.1 0.7 copy-done.4
  4.8 0.0 copy-start.6
  4.8 0.7 copy-done.6
  5.4 0.0 copy-start.7
  5.4 0.7 copy-done.7
  6.1 73.4 %shard_map.121 = (f32[1,2048]{1,0:T(1,128)S(1)}, f32[192,512]{1,0:T(8,128)S(1)}, f32[192,512]{1,0:T(8,128)S(1)}) custom-call(bf16[192,2048]{1,0:T(8,128)(2,1)S(1)} %copy-done, s32[16,2048]{1,0:T(8,128)S(1)} %copy-done.1, s32[1,2048]{1,0:T(1,128)S(1)} %bitcast.7, s32[1,1024]{1,0:T(1,128)S(1)} %bitcast.10, s32[1,2048]{1,0:T(1,128)S(1)} %bitcast.8, ...), custom_call_target="tpu_custom_call" | custom-call | tf_op jit(solution)/shard_map/pallas_call | solution.py:338
  79.6 0.6 copy.16
  80.2 0.7 copy.17
  80.9 0.7 copy.18
Async XLA Ops:
  0.6 0.7 copy-start.2
  0.6 0.7 copy-start.5
  1.3 1.1 %copy-start = (bf16[192,2048]{1,0:T(8,128)(2,1)S(1)}, bf16[192,2048]{1,0:T(8,128)(2,1)}, u32[]{:S(2)}) copy-start(bf16[192,2048]{1,0:T(8,128)(2,1)} %feat_ref.1) | copy-start | bytes 2359300
  2.5 0.9 %copy-start.1 = (s32[16,2048]{1,0:T(8,128)S(1)}, s32[16,2048]{1,0:T(8,128)}, u32[]{:S(2)}) copy-start(s32[16,2048]{1,0:T(8,128)} %neigh_ref.1) | copy-start | bytes 393220
  3.4 0.7 copy-start.3
  4.1 0.7 copy-start.4
  4.8 0.7 copy-start.6
  5.4 0.7 copy-start.7
